TPU v7x, 32 devices: a whole 2x2x4 slice. The times are simulated.
32 devices in a mesh: head: 2 (over y), seq: 16 (over z, x, core).
Axes of the slice: x: 2, y: 2, z: 4, core: 2. Of those that a mesh axis runs over, the one named last changes fastest.
Arguments:
- queries: bfloat16 [16384, 2048], P('seq', 'head'), may hold values from -24 to 24
- key_rows: bfloat16 [16384, 2048], P('seq', 'head'), may hold values from -24 to 24
- value_rows: bfloat16 [16384, 2048], P('seq', 'head'), may hold values from -6 to 6
- token_rates: float32 [4, 16384], P('head', 'seq'), may hold values from 0.01 to 1
- gate_fast: float32 [4, 512, 512], P('head'), may hold values from -0.25 to 0.25
- lift_fast: float32 [4, 512, 512], P('head'), may hold values from -0.25 to 0.25
- down_fast: float32 [4, 512, 512], P('head'), may hold values from -0.25 to 0.25
- memory_gain: float32 [4, 512], P('head'), may hold values from 0.1 to 1
- out_weight: bfloat16 [2048, 2048], P('head'), may hold values from -0.125 to 0.125
Outputs:
- layer_out: bfloat16 [16384, 2048], P('seq', 'head')
All inputs are finite; a program needn't handle non-finite values.
Results may differ from a plain program's by a relative error of at most 0.014.
Values may be sent and summed in bfloat16 or wider, within the bound.
A program may use at most 128 MiB of HBM per device.

v0:
```python
import functools

import jax
import jax.numpy as jnp
from jax import lax
from jax.experimental import pallas as pl
from jax.experimental.pallas import tpu as pltpu
from jax.sharding import PartitionSpec as P

HEAD = 512
WINDOW = 1024
NS_STEPS = 2
COEF_A = 3.4445
COEF_B = -4.775
COEF_C = 2.0315
EPSILON = 1e-06
MESH = pl.DeviceIdType.MESH
F32 = jnp.float32
BF16 = jnp.bfloat16
MASKED = -1e30


def dot(a, b, ca=1, cb=0):
    return lax.dot_general(a, b, (((ca,), (cb,)), ((), ())), preferred_element_type=F32)


def kernel(
    n, tokens, heads, out_cols,
    q_ref, k_ref, v_ref, rate_ref, gate_ref, lift_ref, down_ref, gain_ref, ow_ref, o_ref,
    ek, ev, grad, core_send, core_recv, rs_send, rs_recv, gsum, att, m_ref, l_ref, new_w,
    psend, precv,
    halo_s, halo_r, core_s, core_r, rs_s, rs_r, ag_s, ag_r, nw_s, nw_r, y_s, y_r,
):
    me = lax.axis_index("seq")
    y = lax.axis_index("head")
    rows3 = 3 * HEAD
    core = me % 2
    steps = []
    d = 2
    while d < n:
        steps.append(d)
        d *= 2
    steps = steps[1:] + steps[:1]

    def bit(d):
        return (me // d) % 2

    def partner(d):
        return me + d * (1 - 2 * bit(d))

    barrier = pltpu.get_barrier_semaphore()
    peers = [{"seq": (me + 1) % n}, {"seq": (me + n - 1) % n}, {"head": 1 - y}]
    peers += [{"seq": partner(d)} for d in [1] + steps]
    for peer in peers:
        pl.semaphore_signal(barrier, inc=1, device_id=peer, device_id_type=MESH)
    pl.semaphore_wait(barrier, len(peers))

    def halo_copies(h):
        cols = pl.ds(h * HEAD, HEAD)
        return [
            pltpu.make_async_remote_copy(
                src_ref=src.at[:, cols], dst_ref=dst.at[:, cols],
                send_sem=halo_s.at[2 * h + j], recv_sem=halo_r.at[2 * h + j],
                device_id={"seq": (me + 1) % n}, device_id_type=MESH,
            )
            for j, (src, dst) in enumerate(((k_ref, ek), (v_ref, ev)))
        ]

    @pl.when(me < n - 1)
    def _():
        for h in range(heads):
            for c in halo_copies(h):
                c.start()

    chunk = 256
    tchunks = tokens // chunk

    def gradients(h):
        cols = pl.ds(pl.multiple_of(h * HEAD, HEAD), HEAD)
        grad[h] = jnp.zeros((rows3, HEAD), F32)
        gw = gate_ref[h].astype(BF16)
        lw = lift_ref[h].astype(BF16)
        dw = down_ref[h].astype(BF16)
        gchunk = 512

        def body(i, carry):
            rows = pl.ds(pl.multiple_of(i * gchunk, gchunk), gchunk)
            kk = k_ref[rows, cols]
            vv = v_ref[rows, cols].astype(F32)
            rr = rate_ref[rows, :]
            pick = lax.broadcasted_iota(jnp.int32, rr.shape, 1) == h
            rate = jnp.sum(jnp.where(pick, rr, 0.0), axis=1, keepdims=True)
            target = (-rate * vv).astype(BF16)
            gp = dot(kk, gw)
            lp = dot(kk, lw)
            sg = jax.nn.sigmoid(gp)
            act = gp * sg
            hidden = (act * lp).astype(BF16)
            grad[h, 2 * HEAD : 3 * HEAD, :] += dot(hidden, target, 0, 0)
            bh = dot(target, dw, 1, 1)
            bg = (bh * lp * sg * (1.0 + gp * (1.0 - sg))).astype(BF16)
            bl = (bh * act).astype(BF16)
            grad[h, 0:HEAD, :] += dot(kk, bg, 0, 0)
            grad[h, HEAD : 2 * HEAD, :] += dot(kk, bl, 0, 0)
            return carry

        lax.fori_loop(0, tokens // gchunk, body, 0)

    scale = HEAD ** (-0.5)

    def local_attention(h):
        cols = pl.ds(h * HEAD, HEAD)
        for i in range(tchunks):
            rows = pl.ds(i * chunk, chunk)
            span = (i + 1) * chunk
            s = dot(q_ref[rows, cols], k_ref[0:span, cols], 1, 1) * scale
            qi = lax.broadcasted_iota(jnp.int32, s.shape, 0) + i * chunk
            ki = lax.broadcasted_iota(jnp.int32, s.shape, 1)
            s = jnp.where(ki <= qi, s, MASKED)
            m = jnp.max(s, axis=1, keepdims=True)
            p = jnp.exp(s - m)
            m_ref[h, rows, :] = m
            l_ref[h, rows, :] = jnp.sum(p, axis=1, keepdims=True)
            att[rows, cols] = dot(p.astype(BF16), v_ref[0:span, cols])

    def halo_attention(h):
        cols = pl.ds(h * HEAD, HEAD)

        @pl.when(me > 0)
        def _():
            for c in halo_copies(h):
                c.wait_recv()
            for i in range(tchunks):
                rows = pl.ds(i * chunk, chunk)
                keys = pl.ds(i * chunk, WINDOW - i * chunk)
                s = dot(q_ref[rows, cols], ek[keys, cols], 1, 1) * scale
                qi = lax.broadcasted_iota(jnp.int32, s.shape, 0)
                ki = lax.broadcasted_iota(jnp.int32, s.shape, 1)
                s = jnp.where(ki > qi, s, MASKED)
                m_old = m_ref[h, rows, :]
                m = jnp.maximum(m_old, jnp.max(s, axis=1, keepdims=True))
                p = jnp.exp(s - m)
                fix = jnp.exp(m_old - m)
                l_ref[h, rows, :] = l_ref[h, rows, :] * fix + jnp.sum(p, axis=1, keepdims=True)
                att[rows, cols] = att[rows, cols] * fix + dot(p.astype(BF16), ev[keys, cols])

    gradients(1 - core)
    core_send[...] = grad[1 - core].astype(BF16)
    core_copy = pltpu.make_async_remote_copy(
        src_ref=core_send, dst_ref=core_recv, send_sem=core_s, recv_sem=core_r,
        device_id={"seq": partner(1)}, device_id_type=MESH,
    )
    core_copy.start()
    gradients(core)
    core_copy.wait()

    work = [lambda: local_attention(0), lambda: local_attention(1)]
    late = [lambda: halo_attention(0), lambda: halo_attention(1)]
    off = 0 * me
    size = rows3
    base = 0
    spans = []
    previous = None
    for t, d in enumerate(steps):
        half = size // 2
        keep = pl.multiple_of(off + bit(d) * half, 16)
        give = pl.multiple_of(off + (1 - bit(d)) * half, 16)
        for at in (give, keep):
            r = pl.ds(at, half)
            if t == 0:
                grad[core, r, :] += core_recv[r, :].astype(F32)
            else:
                pr = pl.ds(pl.multiple_of(at - off, 16) + previous, half)
                grad[core, r, :] += rs_recv[pr, :].astype(F32)
            if at is give:
                rs_send[base : base + half, :] = grad[core, r, :].astype(BF16)
                copy = pltpu.make_async_remote_copy(
                    src_ref=rs_send.at[base : base + half], dst_ref=rs_recv.at[base : base + half],
                    send_sem=rs_s.at[t], recv_sem=rs_r.at[t],
                    device_id={"seq": partner(d)}, device_id_type=MESH,
                )
                copy.start()
        if work:
            work.pop(0)()
        copy.wait()
        spans.append((off, size))
        off, size = keep, half
        previous = base
        base += half
    own = pl.ds(off, size)
    gsum[own, :] = (
        grad[core, own, :] + rs_recv[previous : previous + size, :].astype(F32)
    ).astype(BF16)
    for t in reversed(range(len(steps))):
        d = steps[t]
        mine = pl.ds(off, size)
        copy = pltpu.make_async_remote_copy(
            src_ref=gsum.at[mine], dst_ref=gsum.at[mine],
            send_sem=ag_s.at[t], recv_sem=ag_r.at[t],
            device_id={"seq": partner(d)}, device_id_type=MESH,
        )
        copy.start()
        if work:
            work.pop(0)()
        elif late and t < 2:
            late.pop(0)()
        copy.wait()
        off, size = spans[t]
    eye = (
        lax.broadcasted_iota(jnp.int32, (HEAD, HEAD), 0)
        == lax.broadcasted_iota(jnp.int32, (HEAD, HEAD), 1)
    )
    for w, w_ref in enumerate((gate_ref, lift_ref, down_ref)):
        g = gsum[w * HEAD : (w + 1) * HEAD, :].astype(F32)
        trace = jnp.sum(jnp.sum(g * g, axis=1, keepdims=True), axis=0, keepdims=True) + EPSILON
        x = (g * lax.rsqrt(trace)).astype(BF16)
        for sweep in range(NS_STEPS):
            a = dot(x, x, 0, 0)
            b = a.astype(BF16)
            poly = COEF_B * a + COEF_C * dot(b, b) + jnp.where(eye, COEF_A, 0.0)
            x = dot(x, poly.astype(BF16)).astype(BF16)
        old = w_ref[core]
        change = old - x.astype(F32)
        old_sq = jnp.sum(old * old, axis=0, keepdims=True)
        new_sq = jnp.sum(change * change, axis=0, keepdims=True)
        new_w[core, w] = (change * jnp.sqrt(old_sq / (new_sq + EPSILON))).astype(BF16)
    nw_copy = pltpu.make_async_remote_copy(
        src_ref=new_w.at[core], dst_ref=new_w.at[core], send_sem=nw_s, recv_sem=nw_r,
        device_id={"seq": partner(1)}, device_id_type=MESH,
    )
    nw_copy.start()
    for f in work + late:
        f()
    nw_copy.wait()

    y_copies = []
    for i in range(tchunks):
        rows = pl.ds(i * chunk, chunk)
        parts = []
        for h in range(heads):
            cols = pl.ds(h * HEAD, HEAD)
            qq = q_ref[rows, cols]
            gp = dot(qq, new_w[h, 0])
            lp = dot(qq, new_w[h, 1])
            hid = (gp * jax.nn.sigmoid(gp) * lp).astype(BF16)
            mem = dot(hid, new_w[h, 2])
            ms = jnp.mean(mem * mem, axis=1, keepdims=True)
            normed = mem * lax.rsqrt(ms + EPSILON) * gain_ref[h : h + 1, :]
            parts.append((att[rows, cols] / l_ref[h, rows, :] + normed).astype(BF16))
        theirs = pl.ds(pl.multiple_of((1 - y) * out_cols, out_cols), out_cols)
        ours = pl.ds(pl.multiple_of(y * out_cols, out_cols), out_cols)

        def project(cs):
            total = dot(parts[0], ow_ref[0:HEAD, cs])
            for h in range(1, heads):
                total += dot(parts[h], ow_ref[h * HEAD : (h + 1) * HEAD, cs])
            return total

        psend[rows, :] = project(theirs).astype(BF16)
        copy = pltpu.make_async_remote_copy(
            src_ref=psend.at[rows], dst_ref=precv.at[rows], send_sem=y_s.at[i],
            recv_sem=y_r.at[i], device_id={"head": 1 - y}, device_id_type=MESH,
        )
        copy.start()
        y_copies.append(copy)
        o_ref[rows, :] = project(ours).astype(BF16)
    for i in range(tchunks):
        rows = pl.ds(i * chunk, chunk)
        y_copies[i].wait()
        o_ref[rows, :] = (o_ref[rows, :].astype(F32) + precv[rows, :].astype(F32)).astype(BF16)

    @pl.when(me < n - 1)
    def _():
        for h in range(heads):
            for c in halo_copies(h):
                c.wait_send()


def solution(mesh):
    n = mesh.shape["seq"]
    groups = mesh.shape["head"]

    def shards(q, k, v, rates, gate, lift, down, gain, ow):
        tokens, width = q.shape
        heads = gate.shape[0]
        out_cols = ow.shape[1] // groups
        assert heads == 2 and groups == 2 and tokens == WINDOW
        rows3 = 3 * HEAD
        nsteps = n.bit_length() - 2
        dma = pltpu.SemaphoreType.DMA
        return pl.pallas_call(
            functools.partial(kernel, n, tokens, heads, out_cols),
            out_shape=jax.ShapeDtypeStruct((tokens, out_cols), BF16),
            in_specs=[pl.BlockSpec(memory_space=pltpu.VMEM)] * 9,
            out_specs=pl.BlockSpec(memory_space=pltpu.VMEM),
            scratch_shapes=[
                pltpu.VMEM((tokens, width), BF16),
                pltpu.VMEM((tokens, width), BF16),
                pltpu.VMEM((heads, rows3, HEAD), F32),
                pltpu.VMEM((rows3, HEAD), BF16),
                pltpu.VMEM((rows3, HEAD), BF16),
                pltpu.VMEM((rows3, HEAD), BF16),
                pltpu.VMEM((rows3, HEAD), BF16),
                pltpu.VMEM((rows3, HEAD), BF16),
                pltpu.VMEM((tokens, width), F32),
                pltpu.VMEM((heads, tokens, 1), F32),
                pltpu.VMEM((heads, tokens, 1), F32),
                pltpu.VMEM((heads, 3, HEAD, HEAD), BF16),
                pltpu.VMEM((tokens, out_cols), BF16),
                pltpu.VMEM((tokens, out_cols), BF16),
                dma((2 * heads,)), dma((2 * heads,)),
                dma, dma,
                dma((nsteps,)), dma((nsteps,)),
                dma((nsteps,)), dma((nsteps,)),
                dma, dma,
                dma((tokens // 256,)), dma((tokens // 256,)),
            ],
            compiler_params=pltpu.CompilerParams(
                collective_id=0, has_side_effects=True, vmem_limit_bytes=62 * 1024 * 1024
            ),
            cost_estimate=pl.CostEstimate(
                flops=30 * 10**9, bytes_accessed=20 * 2**20, transcendentals=10**7
            ),
        )(q, k, v, rates.T, gate, lift, down, gain, ow)

    return jax.shard_map(
        shards,
        mesh=mesh,
        in_specs=(
            P("seq", "head"),
            P("seq", "head"),
            P("seq", "head"),
            P("head", "seq"),
            P("head", None, None),
            P("head", None, None),
            P("head", None, None),
            P("head", None),
            P("head", None),
        ),
        out_specs=P("seq", "head"),
        check_vma=False,
    )
```

profile of v0, /device:TPU:0, one launch (start us, length us, event | category | flops | bytes accessed | tf_op | source)
XLA Modules:
  0.0 183.9 jit_solution(7404777328902680725)
XLA Ops:
  0.0 1.7 copy.10
  1.7 179.1 %shard_map.91 = bf16[1024,1024]{1,0:T(8,128)(2,1)} custom-call(bf16[1024,1024]{1,0:T(8,128)(2,1)} %q_ref.1, bf16[1024,1024]{1,0:T(8,128)(2,1)} %k_ref.1, bf16[1024,1024]{1,0:T(8,128)(2,1)} %v_ref.1, f32[1024,2]{1,0:T(8,128)} %bitcast.1, f32[2,512,512]{2,1,0:T(8,128)} %gate_ref.1, f32[2,512,512]{2,1,0:T(8,128)} %lift_ref.1, f32[2,512,512]{2,1,0:T(8,128)} %down_ref.1, ...), custom_call_target="tpu_custom_call" | custom-call | flops 30000001024 | bytes 20971520 | tf_op jit(solution)/shard_map/pallas_call | solution.py:291
  180.8 3.1 %copy.12 = bf16[1024,1024]{1,0:T(8,128)(2,1)} copy(bf16[1024,1024]{1,0:T(8,128)(2,1)} %shard_map.91) | data formatting | bytes 4194304
where the time goes:
time: 184 us
  Pallas kernels  179 us (97%)
  local copies, waits for them, and re-layouts  4.8 us (3%)
    pallas_call x1, Pallas kernels, shards(): pl.pallas_call(functools.partial(kernel, n, tokens, heads, out_cols), out...  179 us
    unnamed x2, local copies, waits for them, and re-layouts  4.8 us

commit v1 on v0

--- a/solution.py
+++ b/solution.py
@@ -40,7 +40,8 @@
     while d < n:
         steps.append(d)
         d *= 2
-    steps = steps[1:] + steps[:1]
+    nsteps = len(steps)
+    orders = [steps, steps[1:] + steps[:1], steps[:1] + steps[:0:-1]]
 
     def bit(d):
         return (me // d) % 2
@@ -55,25 +56,29 @@
         pl.semaphore_signal(barrier, inc=1, device_id=peer, device_id_type=MESH)
     pl.semaphore_wait(barrier, len(peers))
 
-    def halo_copies(h):
-        cols = pl.ds(h * HEAD, HEAD)
+    chunk = 256
+    tchunks = tokens // chunk
+
+    def halo_copies(c):
+        rows = pl.ds(c * chunk, chunk)
         return [
             pltpu.make_async_remote_copy(
-                src_ref=src.at[:, cols], dst_ref=dst.at[:, cols],
-                send_sem=halo_s.at[2 * h + j], recv_sem=halo_r.at[2 * h + j],
+                src_ref=src.at[rows], dst_ref=dst.at[rows],
+                send_sem=halo_s.at[2 * c + j], recv_sem=halo_r.at[2 * c + j],
                 device_id={"seq": (me + 1) % n}, device_id_type=MESH,
             )
             for j, (src, dst) in enumerate(((k_ref, ek), (v_ref, ev)))
         ]
 
-    @pl.when(me < n - 1)
-    def _():
-        for h in range(heads):
-            for c in halo_copies(h):
-                c.start()
-
-    chunk = 256
-    tchunks = tokens // chunk
+    def start_halo(chunks):
+        @pl.when(me < n - 1)
+        def _():
+            for c in chunks:
+                for copy in halo_copies(c):
+                    copy.start()
+
+    early = tchunks // 2
+    start_halo(range(tchunks - 1, early - 1, -1))
 
     def gradients(h):
         cols = pl.ds(pl.multiple_of(h * HEAD, HEAD), HEAD)
@@ -123,16 +128,15 @@
             l_ref[h, rows, :] = jnp.sum(p, axis=1, keepdims=True)
             att[rows, cols] = dot(p.astype(BF16), v_ref[0:span, cols])
 
-    def halo_attention(h):
-        cols = pl.ds(h * HEAD, HEAD)
-
+    def halo_attention(i):
         @pl.when(me > 0)
         def _():
-            for c in halo_copies(h):
+            for c in halo_copies(i):
                 c.wait_recv()
-            for i in range(tchunks):
-                rows = pl.ds(i * chunk, chunk)
-                keys = pl.ds(i * chunk, WINDOW - i * chunk)
+            rows = pl.ds(i * chunk, chunk)
+            keys = pl.ds(i * chunk, WINDOW - i * chunk)
+            for h in range(heads):
+                cols = pl.ds(h * HEAD, HEAD)
                 s = dot(q_ref[rows, cols], ek[keys, cols], 1, 1) * scale
                 qi = lax.broadcasted_iota(jnp.int32, s.shape, 0)
                 ki = lax.broadcasted_iota(jnp.int32, s.shape, 1)
@@ -155,62 +159,76 @@
     core_copy.wait()
 
     work = [lambda: local_attention(0), lambda: local_attention(1)]
-    late = [lambda: halo_attention(0), lambda: halo_attention(1)]
-    off = 0 * me
-    size = rows3
-    base = 0
-    spans = []
-    previous = None
-    for t, d in enumerate(steps):
-        half = size // 2
-        keep = pl.multiple_of(off + bit(d) * half, 16)
-        give = pl.multiple_of(off + (1 - bit(d)) * half, 16)
-        for at in (give, keep):
-            r = pl.ds(at, half)
-            if t == 0:
-                grad[core, r, :] += core_recv[r, :].astype(F32)
-            else:
-                pr = pl.ds(pl.multiple_of(at - off, 16) + previous, half)
-                grad[core, r, :] += rs_recv[pr, :].astype(F32)
-            if at is give:
-                rs_send[base : base + half, :] = grad[core, r, :].astype(BF16)
-                copy = pltpu.make_async_remote_copy(
-                    src_ref=rs_send.at[base : base + half], dst_ref=rs_recv.at[base : base + half],
-                    send_sem=rs_s.at[t], recv_sem=rs_r.at[t],
-                    device_id={"seq": partner(d)}, device_id_type=MESH,
-                )
-                copy.start()
+    late = list(range(tchunks - 1, -1, -1))
+    offs = [w * HEAD + 0 * me for w in range(3)]
+    sizes = [HEAD] * 3
+    bases = [w * HEAD for w in range(3)]
+    previous = [None] * 3
+    spans = [[], [], []]
+    copies = [None] * 3
+    for t in range(nsteps):
+        for w in range(3):
+            d = orders[w][t]
+            off, half, base = offs[w], sizes[w] // 2, bases[w]
+            keep = pl.multiple_of(off + bit(d) * half, 16)
+            give = pl.multiple_of(off + (1 - bit(d)) * half, 16)
+            if t > 0:
+                copies[w].wait()
+            for first, at in ((True, give), (False, keep)):
+                r = pl.ds(at, half)
+                if t == 0:
+                    grad[core, r, :] += core_recv[r, :].astype(F32)
+                else:
+                    pr = pl.ds(pl.multiple_of(at - off, 16) + previous[w], half)
+                    grad[core, r, :] += rs_recv[pr, :].astype(F32)
+                if first:
+                    rs_send[base : base + half, :] = grad[core, r, :].astype(BF16)
+                    copies[w] = pltpu.make_async_remote_copy(
+                        src_ref=rs_send.at[base : base + half],
+                        dst_ref=rs_recv.at[base : base + half],
+                        send_sem=rs_s.at[w * nsteps + t], recv_sem=rs_r.at[w * nsteps + t],
+                        device_id={"seq": partner(d)}, device_id_type=MESH,
+                    )
+                    copies[w].start()
+            spans[w].append((off, sizes[w]))
+            offs[w], sizes[w] = keep, half
+            previous[w] = base
+            bases[w] += half
         if work:
             work.pop(0)()
-        copy.wait()
-        spans.append((off, size))
-        off, size = keep, half
-        previous = base
-        base += half
-    own = pl.ds(off, size)
-    gsum[own, :] = (
-        grad[core, own, :] + rs_recv[previous : previous + size, :].astype(F32)
-    ).astype(BF16)
-    for t in reversed(range(len(steps))):
-        d = steps[t]
-        mine = pl.ds(off, size)
-        copy = pltpu.make_async_remote_copy(
-            src_ref=gsum.at[mine], dst_ref=gsum.at[mine],
-            send_sem=ag_s.at[t], recv_sem=ag_r.at[t],
-            device_id={"seq": partner(d)}, device_id_type=MESH,
-        )
-        copy.start()
+    for t in reversed(range(nsteps)):
+        for w in range(3):
+            copies[w].wait()
+            if t == nsteps - 1:
+                own = pl.ds(offs[w], sizes[w])
+                gsum[own, :] = (
+                    grad[core, own, :]
+                    + rs_recv[previous[w] : previous[w] + sizes[w], :].astype(F32)
+                ).astype(BF16)
+            else:
+                offs[w], sizes[w] = spans[w][t + 1]
+            mine = pl.ds(offs[w], sizes[w])
+            copies[w] = pltpu.make_async_remote_copy(
+                src_ref=gsum.at[mine], dst_ref=gsum.at[mine],
+                send_sem=ag_s.at[w * nsteps + t], recv_sem=ag_r.at[w * nsteps + t],
+                device_id={"seq": partner(orders[w][t])}, device_id_type=MESH,
+            )
+            copies[w].start()
         if work:
             work.pop(0)()
-        elif late and t < 2:
-            late.pop(0)()
-        copy.wait()
-        off, size = spans[t]
+        elif late and late[0] >= early:
+            halo_attention(late.pop(0))
+    for f in work:
+        f()
     eye = (
         lax.broadcasted_iota(jnp.int32, (HEAD, HEAD), 0)
         == lax.broadcasted_iota(jnp.int32, (HEAD, HEAD), 1)
     )
+    nw_copies = []
     for w, w_ref in enumerate((gate_ref, lift_ref, down_ref)):
+        copies[w].wait()
+        if w == 2:
+            start_halo(range(early - 1, -1, -1))
         g = gsum[w * HEAD : (w + 1) * HEAD, :].astype(F32)
         trace = jnp.sum(jnp.sum(g * g, axis=1, keepdims=True), axis=0, keepdims=True) + EPSILON
         x = (g * lax.rsqrt(trace)).astype(BF16)
@@ -224,17 +242,20 @@
         old_sq = jnp.sum(old * old, axis=0, keepdims=True)
         new_sq = jnp.sum(change * change, axis=0, keepdims=True)
         new_w[core, w] = (change * jnp.sqrt(old_sq / (new_sq + EPSILON))).astype(BF16)
-    nw_copy = pltpu.make_async_remote_copy(
-        src_ref=new_w.at[core], dst_ref=new_w.at[core], send_sem=nw_s, recv_sem=nw_r,
-        device_id={"seq": partner(1)}, device_id_type=MESH,
-    )
-    nw_copy.start()
-    for f in work + late:
-        f()
-    nw_copy.wait()
-
-    y_copies = []
-    for i in range(tchunks):
+        nw_copy = pltpu.make_async_remote_copy(
+            src_ref=new_w.at[core, w], dst_ref=new_w.at[core, w],
+            send_sem=nw_s.at[w], recv_sem=nw_r.at[w],
+            device_id={"seq": partner(1)}, device_id_type=MESH,
+        )
+        nw_copy.start()
+        nw_copies.append(nw_copy)
+    for copy in nw_copies:
+        copy.wait()
+
+    y_copies = [None] * tchunks
+    for i in reversed(range(tchunks)):
+        if i in late:
+            halo_attention(i)
         rows = pl.ds(i * chunk, chunk)
         parts = []
         for h in range(heads):
@@ -262,17 +283,17 @@
             recv_sem=y_r.at[i], device_id={"head": 1 - y}, device_id_type=MESH,
         )
         copy.start()
-        y_copies.append(copy)
+        y_copies[i] = copy
         o_ref[rows, :] = project(ours).astype(BF16)
-    for i in range(tchunks):
+    for i in reversed(range(tchunks)):
         rows = pl.ds(i * chunk, chunk)
         y_copies[i].wait()
         o_ref[rows, :] = (o_ref[rows, :].astype(F32) + precv[rows, :].astype(F32)).astype(BF16)
 
     @pl.when(me < n - 1)
     def _():
-        for h in range(heads):
-            for c in halo_copies(h):
+        for i in range(tchunks):
+            for c in halo_copies(i):
                 c.wait_send()
 
 
@@ -308,11 +329,11 @@
                 pltpu.VMEM((heads, 3, HEAD, HEAD), BF16),
                 pltpu.VMEM((tokens, out_cols), BF16),
                 pltpu.VMEM((tokens, out_cols), BF16),
-                dma((2 * heads,)), dma((2 * heads,)),
+                dma((2 * tokens // 256,)), dma((2 * tokens // 256,)),
                 dma, dma,
-                dma((nsteps,)), dma((nsteps,)),
-                dma((nsteps,)), dma((nsteps,)),
-                dma, dma,
+                dma((3 * nsteps,)), dma((3 * nsteps,)),
+                dma((3 * nsteps,)), dma((3 * nsteps,)),
+                dma((3,)), dma((3,)),
                 dma((tokens // 256,)), dma((tokens // 256,)),
             ],
             compiler_params=pltpu.CompilerParams(

time: 184 us -> 163 us (0.89)
  the two profiles are of different devices: /device:TPU:0 before, /device:TPU:16 now
where the time goes in v1:
time: 163 us
  Pallas kernels  158 us (97%)
  local copies, waits for them, and re-layouts  4.8 us (3%)
    pallas_call x1, Pallas kernels, shards(): pl.pallas_call(functools.partial(kernel, n, tokens, heads, out_cols), out...  158 us
    unnamed x2, local copies, waits for them, and re-layouts  4.8 us

profile of v1, /device:TPU:16, one launch (start us, length us, event | category | flops | bytes accessed | tf_op | source)
XLA Modules:
  0.0 162.5 jit_solution(8049696953413833273)
XLA Ops:
  0.0 1.7 %copy.10 = f32[2,1024]{0,1:T(8,128)} copy(f32[2,1024]{1,0:T(2,128)} %param.12) | data formatting | bytes 16384 | tf_op args[3]
  1.7 157.7 %shard_map.91 = bf16[1024,1024]{1,0:T(8,128)(2,1)} custom-call(bf16[1024,1024]{1,0:T(8,128)(2,1)} %q_ref.1, bf16[1024,1024]{1,0:T(8,128)(2,1)} %k_ref.1, bf16[1024,1024]{1,0:T(8,128)(2,1)} %v_ref.1, f32[1024,2]{1,0:T(8,128)} %bitcast.1, f32[2,512,512]{2,1,0:T(8,128)} %gate_ref.1, f32[2,512,512]{2,1,0:T(8,128)} %lift_ref.1, f32[2,512,512]{2,1,0:T(8,128)} %down_ref.1, ...), custom_call_target="tpu_custom_call" | custom-call | flops 30000001024 | bytes 20971520 | tf_op jit(solution)/shard_map/pallas_call | solution.py:312
  159.4 3.1 %copy.12 = bf16[1024,1024]{1,0:T(8,128)(2,1)} copy(bf16[1024,1024]{1,0:T(8,128)(2,1)} %shard_map.91) | data formatting | bytes 4194304

commit v2 on v1

--- a/solution.py
+++ b/solution.py
@@ -41,7 +41,7 @@
         steps.append(d)
         d *= 2
     nsteps = len(steps)
-    orders = [steps, steps[1:] + steps[:1], steps[:1] + steps[:0:-1]]
+    orders = [steps[i:] + steps[:i] for i in (0, 1, 2)]
 
     def bit(d):
         return (me // d) % 2
@@ -77,7 +77,7 @@
                 for copy in halo_copies(c):
                     copy.start()
 
-    early = tchunks // 2
+    early = 3*tchunks//4
     start_halo(range(tchunks - 1, early - 1, -1))
 
     def gradients(h):

time: 163 us -> 133 us (0.82)
  the two profiles are of different devices: /device:TPU:16 before, /device:TPU:0 now
where the time goes in v2:
time: 133 us; the launch traced here: 131 us
  Pallas kernels  127 us (95%)
  local copies, waits for them, and re-layouts  4.8 us (4%)
    pallas_call x1, Pallas kernels, shards(): pl.pallas_call(functools.partial(kernel, n, tokens, heads, out_cols), out...  127 us
    unnamed x2, local copies, waits for them, and re-layouts  4.8 us

profile of v2, /device:TPU:0, one launch (start us, length us, event | category | flops | bytes accessed | tf_op | source)
XLA Modules:
  0.0 131.4 jit_solution(17461417173527377946)
XLA Ops:
  0.0 1.7 %copy.10 = f32[2,1024]{0,1:T(8,128)} copy(f32[2,1024]{1,0:T(2,128)} %param.12) | data formatting | bytes 16384 | tf_op args[3]
  1.7 126.5 %shard_map.91 = bf16[1024,1024]{1,0:T(8,128)(2,1)} custom-call(bf16[1024,1024]{1,0:T(8,128)(2,1)} %q_ref.1, bf16[1024,1024]{1,0:T(8,128)(2,1)} %k_ref.1, bf16[1024,1024]{1,0:T(8,128)(2,1)} %v_ref.1, f32[1024,2]{1,0:T(8,128)} %bitcast.1, f32[2,512,512]{2,1,0:T(8,128)} %gate_ref.1, f32[2,512,512]{2,1,0:T(8,128)} %lift_ref.1, f32[2,512,512]{2,1,0:T(8,128)} %down_ref.1, ...), custom_call_target="tpu_custom_call" | custom-call | flops 30000001024 | bytes 20971520 | tf_op jit(solution)/shard_map/pallas_call | solution.py:312
  128.3 3.1 %copy.12 = bf16[1024,1024]{1,0:T(8,128)(2,1)} copy(bf16[1024,1024]{1,0:T(8,128)(2,1)} %shard_map.91) | data formatting | bytes 4194304
